TPU v7x, 32 devices: a whole 2x2x4 slice. The times are simulated.
32 devices in a mesh: chan: 8 (over z, y), split: 4 (over x, core).
Axes of the slice: x: 2, y: 2, z: 4, core: 2. Of those that a mesh axis runs over, the one named last changes fastest.
Arguments:
- omega: bfloat16 [8, 2048, 2048], P('chan', 'split'), as said below
- hamil: bfloat16 [8, 2048, 2048], P('chan', 'split'), as said below
- pp_sign: float32 [8, 2048], P('chan', 'split'), may hold values from -1 to 1, as said below
- ph_sign: float32 [8, 2048], P('chan', 'split'), may hold values from -1 to 1, as said below
- row_coef: float32 [8, 2048], P('chan', 'split'), may hold values from -2 to 2
- col_coef: float32 [8, 2048], P('chan'), may hold values from -2 to 2
- col_perm: int32 [8, 2048], P('chan'), may hold values from 0 to 2047, each once within a row
- send_order: int32 [8, 2048], P('chan', 'split'), may hold values from 0 to 511, as said below
Outputs:
- z_out: bfloat16 [8, 2048, 2048], P('chan', 'split')
- one_body: float32 [2048], replicated
Inputs may be any that keep to these rules, and one draw needn't show every extreme that they name: omega[c] is antisymmetric for every channel c. hamil[c] is symmetric for every channel c. `pp_sign`: every entry is -1, 0 or 1; nearly all are 1. `ph_sign`: every entry is -1, 0 or 1; each aligned block of 512 entries of a channel holds exactly 32 nonzero entries. `send_order`: for every channel, each aligned block of 512 entries is a permutation of 0 to 511.
All inputs are finite; a program needn't handle non-finite values.
Results may differ from a plain program's by a relative error of at most 0.0034.
Values may be sent and summed in bfloat16 or wider, within the bound.
A program may use at most 128 MiB of HBM per device.

v0:
```python
import math

import jax
import jax.numpy as jnp
from jax import lax
from jax.sharding import PartitionSpec as P


def fold_pair(left_first, left_second, running, fragments):
    leading, trailing = fragments
    running = jnp.dot(left_first, leading, preferred_element_type=jnp.float32)
    return running - jnp.dot(left_second, trailing, preferred_element_type=jnp.float32)


def on_device(omega, hamil, pp_sign, ph_sign, row_coef, col_coef, col_perm, send_order):
    chan_count = lax.axis_size("chan")
    height = omega.shape[1]
    breadth = omega.shape[2]
    slots_each = height // chan_count
    omega_rows = omega[0]
    hamil_rows = hamil[0]
    pp_rows = pp_sign[0]
    chan_index = lax.axis_index("chan")
    degeneracy = (2 * (chan_index // 2) + 1).astype(jnp.float32)
    weight_sq = sum(((2 * (chan_pos // 2) + 1) ** 2 for chan_pos in range(chan_count)))
    norm_factor = 1.0 / math.sqrt(breadth * weight_sq)
    zeros_block = jnp.zeros((height, breadth), jnp.float32)
    scaled_h = (pp_rows[:, None] * hamil_rows).astype(jnp.bfloat16)
    half_rows = jnp.dot(
        omega_rows,
        lax.all_gather(scaled_h, "split", axis=0, tiled=True),
        preferred_element_type=jnp.float32,
    )
    flipped = lax.all_to_all(half_rows, "split", split_axis=1, concat_axis=0, tiled=True)
    ladder = half_rows + flipped.T
    order_rows = send_order[0]
    sorted_o = jnp.take(omega_rows, order_rows, axis=0).reshape(chan_count, slots_each, breadth)
    sorted_h = jnp.take(hamil_rows, order_rows, axis=0).reshape(chan_count, slots_each, breadth)
    got_o, got_h = (
        lax.all_to_all(sorted_o, "chan", split_axis=0, concat_axis=0, tiled=True),
        lax.all_to_all(sorted_h, "chan", split_axis=0, concat_axis=0, tiled=True),
    )
    recv_o = got_o.reshape(height, breadth)
    recv_h = got_h.reshape(height, breadth)
    perm_cols = col_perm[0]
    coefs = row_coef[0][:, None] * col_coef[0][None, :]
    bar_o = (coefs * jnp.take(recv_o, perm_cols, axis=1)).astype(jnp.bfloat16)
    bar_h = (coefs * jnp.take(recv_h, perm_cols, axis=1)).astype(jnp.bfloat16)
    row_signs = ph_sign[0][:, None]
    right_o = (row_signs * bar_o).astype(jnp.bfloat16)
    right_h = (row_signs * bar_h).astype(jnp.bfloat16)
    ph_sum = fold_pair(
        bar_o,
        bar_h,
        zeros_block,
        (
            lax.all_gather(right_h, "split", axis=0, tiled=True),
            lax.all_gather(right_o, "split", axis=0, tiled=True),
        ),
    )
    inverse_cols = (
        jnp.zeros((breadth,), jnp.int32).at[perm_cols].set(jnp.arange(breadth, dtype=jnp.int32))
    )
    back = jnp.take(coefs * ph_sum, inverse_cols, axis=1).astype(jnp.bfloat16)
    returned = lax.all_to_all(
        back.reshape(chan_count, slots_each, breadth),
        "chan",
        split_axis=0,
        concat_axis=0,
        tiled=True,
    )
    inverse_rows = (
        jnp.zeros((height,), jnp.int32).at[order_rows].set(jnp.arange(height, dtype=jnp.int32))
    )
    placed = jnp.take(returned.reshape(height, breadth), inverse_rows, axis=0)
    combined = ladder + placed.astype(jnp.float32)
    local_part = degeneracy * jnp.dot(pp_rows, combined, precision=lax.Precision.HIGHEST)
    one_body = lax.psum(local_part, ("chan", "split")) * norm_factor
    return (combined.astype(jnp.bfloat16)[None], one_body)


def solution(mesh):
    in_specs = (
        P("chan", "split", None),
        P("chan", "split", None),
        P("chan", "split"),
        P("chan", "split"),
        P("chan", "split"),
        P("chan", None),
        P("chan", None),
        P("chan", "split"),
    )
    out_specs = (P("chan", "split", None), P())
    return jax.shard_map(
        on_device, mesh=mesh, in_specs=in_specs, out_specs=out_specs, check_vma=False
    )
```

profile of v0, /device:TPU:0, one launch (start us, length us, event | category | flops | bytes accessed | tf_op | source)
XLA Modules:
  0.0 476.0 jit_solution(6509289069803459065)
XLA Ops:
  12.1 7.1 %gather_fusion.3 = bf16[512,2048]{1,0:T(8,128)(2,1)} fusion(bf16[512,2048]{1,0:T(8,128)(2,1)} %bitcast.59, s32[1024]{0:T(1024)S(1)} %pad_clamp_fusion.1), kind=kCustom, calls=%fused_computation.2.clone | custom fusion | bytes 4196352 | tf_op jit(solution)/shard_map/jit(_take)/gather | solution.py:38
  19.2 4.0 broadcast_select_fusion.1
  23.1 55.4 %all_to_all.34 = bf16[8,64,2048]{2,1,0:T(8,128)(2,1)} all-to-all(bf16[8,64,2048]{2,1,0:T(8,128)(2,1)S(1)} %bitcast.65), channel_id=1, replica_groups=mesh['chan'=8,'split'=4] {'chan'}, dimensions={0} | all-to-all | bytes 4194304 | tf_op jit(solution)/shard_map/all_to_all | solution.py:40
  78.6 4.5 all-to-all-start.2
  83.1 3.9 copy.20
  87.1 11.1 %gather_fusion.2 = bf16[2048,512]{1,0:T(8,128)(2,1)} fusion(bf16[512,2048]{0,1:T(8,128)(2,1)} %copy.20, s32[2048]{0:T(1024)S(1)} %fusion.7), kind=kCustom, calls=%fused_computation.1.clone | custom fusion | bytes 4202496 | tf_op jit(solution)/shard_map/jit(_take)/gather | solution.py:47
  98.2 4.0 copy.21
  102.2 28.3 %all-to-all-done.2 = bf16[8,64,2048]{2,1,0:T(8,128)(2,1)} async-done(((bf16[8,64,2048]{2,1,0:T(8,128)(2,1)}), bf16[8,64,2048]{2,1,0:T(8,128)(2,1)}, u32[]{:S(2)}, u32[]{:S(2)}) %all-to-all-start.2) | async-done | bytes 2097184 | tf_op jit(solution)/shard_map/all_to_all | solution.py:41
  130.4 3.9 copy.22
  134.4 11.1 %gather_fusion.4 = bf16[2048,512]{1,0:T(8,128)(2,1)} fusion(bf16[512,2048]{0,1:T(8,128)(2,1)} %copy.22, s32[2048]{0:T(1024)S(1)} %fusion.7), kind=kCustom, calls=%fused_computation.4.clone | custom fusion | bytes 4202496 | tf_op jit(solution)/shard_map/jit(_take)/gather | solution.py:48
  145.4 3.9 copy.23
  149.4 5.7 %multiply_convert_fusion = (bf16[512,2048]{1,0:T(8,128)(2,1)}, bf16[512,2048]{1,0:T(8,128)(2,1)}) fusion(f32[512]{0:T(512)S(1)} %bitcast.76, bf16[2048,512]{0,1:T(8,128)(2,1)} %copy.21, pred[2048]{0:T(1024)(128)(4,1)S(1)} %compare_and_fusion, f32[2048]{0:T(1024)S(1)} %bitcast.71, f32[512]{0:T(512)S(1)} %bitcast.77, bf16[2048,512]{0,1:T(8,128)(2,1)} %copy.23), kind=kLoop, calls=%fused_computation.16 | loop fusion | flops 15728640 | bytes 8402944 | tf_op jit(solution)/shard_map/convert_element_type | solution.py:50
  159.4 8.2 %scatter_custom_fusion = s32[2048]{0:T(1024)S(1)} fusion(s32[2048]{0:T(1024)S(1)} %bitcast.75, s32[2048]{0:T(1024)S(1)} %iota.6, s32[]{:T(128)} %constant.38.clone.1), kind=kCustom, calls=%fused_computation.37 | custom fusion | bytes 8196 | tf_op jit(solution)/shard_map/scatter | solution.py:62
  167.6 45.0 %all-gather.6.cloned.1.call-done = bf16[2048,2048]{1,0:T(8,128)(2,1)} async-done(((bf16[512,2048]{1,0:T(8,128)(2,1)}), bf16[2048,2048]{1,0:T(8,128)(2,1)}) %all-gather.6.cloned.1.call-update) | async-done | bytes 8388624 | tf_op jit(solution)/shard_map/all_gather | solution.py:57
  212.6 10.7 %fusion.4 = f32[512,2048]{1,0:T(8,128)} fusion(bf16[2048,2048]{1,0:T(8,128)(2,1)} %all-gather.6.cloned.1.call-done, bf16[2048,512]{0,1:T(8,128)(2,1)} %copy.21, f32[2048]{0:T(1024)S(1)} %bitcast.72, f32[512]{0:T(512)S(1)} %bitcast.78, pred[2048]{0:T(1024)(128)(4,1)S(1)} %compare_and_fusion), kind=kOutput, calls=%fused_computation.22 | convolution fusion | flops 4300210176 | bytes 14692352 | tf_op jit(solution)/shard_map/dot_general | solution.py:11
  223.3 49.2 %all-gather.8.cloned.1.call-done = bf16[2048,2048]{1,0:T(8,128)(2,1)} async-done(((bf16[512,2048]{1,0:T(8,128)(2,1)}), bf16[2048,2048]{1,0:T(8,128)(2,1)}) %all-gather.8.cloned.1.call-update) | async-done | bytes 8388624 | tf_op jit(solution)/shard_map/all_gather | solution.py:58
  272.5 11.1 %multiply_multiply_fusion = bf16[512,2048]{1,0:T(8,128)(2,1)} fusion(f32[512,2048]{1,0:T(8,128)} %fusion.4, bf16[2048,2048]{1,0:T(8,128)(2,1)} %all-gather.8.cloned.1.call-done, f32[2048]{0:T(1024)S(1)} %bitcast.73, f32[512]{0:T(512)S(1)} %bitcast.79, bf16[2048,512]{0,1:T(8,128)(2,1)} %copy.23, pred[2048]{0:T(1024)(128)(4,1)S(1)} %compare_and_fusion), kind=kOutput, calls=%fused_computation.8 | convolution fusion | flops 4304404480 | bytes 16789504 | tf_op jit(solution)/shard_map/dot_general | solution.py:12
  283.6 4.0 copy.24
  287.6 11.1 %gather_fusion = bf16[2048,512]{1,0:T(8,128)(2,1)} fusion(bf16[512,2048]{0,1:T(8,128)(2,1)} %copy.24, s32[2048]{0:T(1024)S(1)} %fusion.6), kind=kCustom, calls=%fused_computation.5 | custom fusion | bytes 4202496 | tf_op jit(solution)/shard_map/jit(_take)/gather | solution.py:64
  298.7 3.9 copy.25
  306.1 5.6 %all-to-all-start.3 = ((bf16[8,64,2048]{2,1,0:T(8,128)(2,1)}), bf16[8,64,2048]{2,1,0:T(8,128)(2,1)}, u32[]{:S(2)}, u32[]{:S(2)}) async-start(bf16[8,64,2048]{2,1,0:T(8,128)(2,1)} %select_convert_fusion), calls=%async_computation.3 | async-start | bytes 4194304 | tf_op jit(solution)/shard_map/all_to_all | solution.py:65
  311.8 20.6 %all-gather.4.cloned.1.call-done = bf16[2048,2048]{1,0:T(8,128)(2,1)} async-done(((bf16[512,2048]{1,0:T(8,128)(2,1)}), bf16[2048,2048]{1,0:T(8,128)(2,1)}) %all-gather.4.cloned.1.call-update) | async-done | bytes 8388624 | tf_op jit(solution)/shard_map/all_gather | solution.py:31
  332.4 9.7 %fusion.14 = f32[2048,512]{1,0:T(8,128)} fusion(bf16[2048,2048]{1,0:T(8,128)(2,1)} %all-gather.4.cloned.1.call-done, bf16[1,512,2048]{2,1,0:T(8,128)(2,1)S(1)} %copy-done), kind=kOutput, calls=%fused_computation.45 | convolution fusion | flops 4294967296 | bytes 14680064 | tf_op jit(solution)/shard_map/dot_general | solution.py:29
  342.1 5.3 %copy.19 = f32[512,4,512]{2,0,1:T(8,128)} copy(f32[512,4,512]{0,2,1:T(8,128)} %bitcast.60) | data formatting | bytes 8388608 | tf_op jit(solution)/shard_map/all_to_all | solution.py:34
  347.4 13.1 %all-to-all-done.3 = bf16[8,64,2048]{2,1,0:T(8,128)(2,1)} async-done(((bf16[8,64,2048]{2,1,0:T(8,128)(2,1)}), bf16[8,64,2048]{2,1,0:T(8,128)(2,1)}, u32[]{:S(2)}, u32[]{:S(2)}) %all-to-all-start.3) | async-done | bytes 2097184 | tf_op jit(solution)/shard_map/all_to_all | solution.py:65
  360.5 5.1 %all-to-all-start = ((f32[512,4,512]{2,0,1:T(8,128)}), f32[512,4,512]{2,0,1:T(8,128)}, u32[]{:S(2)}, u32[]{:S(2)}) async-start(f32[512,4,512]{2,0,1:T(8,128)} %copy.19), calls=%async_computation | async-start | bytes 8388608 | tf_op jit(solution)/shard_map/all_to_all | solution.py:34
  368.1 7.1 %gather_fusion.5 = bf16[512,2048]{1,0:T(8,128)(2,1)} fusion(bf16[512,2048]{1,0:T(8,128)(2,1)} %bitcast.25, s32[1024]{0:T(1024)S(1)} %pad_clamp_fusion), kind=kCustom, calls=%fused_computation.3.clone | custom fusion | bytes 4196352 | tf_op jit(solution)/shard_map/jit(_take)/gather | solution.py:75
  375.2 3.9 copy.26
  379.1 34.5 %all-to-all-done = f32[512,4,512]{2,0,1:T(8,128)} async-done(((f32[512,4,512]{2,0,1:T(8,128)}), f32[512,4,512]{2,0,1:T(8,128)}, u32[]{:S(2)}, u32[]{:S(2)}) %all-to-all-start) | async-done | bytes 4194336 | tf_op jit(solution)/shard_map/all_to_all | solution.py:34
  413.6 8.0 %convert_bitcast_fusion = (bf16[1,512,2048]{1,2,0:T(8,128)(2,1)}, f32[512,2048]{0,1:T(8,128)}) fusion(bf16[512,2048]{0,1:T(8,128)(2,1)} %copy.26, pred[512]{0:T(512)(128)(4,1)S(1)} %compare_and_fusion.2, f32[512,4,512]{2,0,1:T(8,128)} %all-to-all-done, f32[2048,512]{1,0:T(8,128)} %fusion.14), kind=kLoop, calls=%fused_computation.19 | loop fusion | flops 5242880 | bytes 16777728 | tf_op jit(solution)/shard_map/broadcast_in_dim | solution.py:79
  425.5 5.7 %fusion.10 = f32[1,2048]{1,0:T(1,128)S(1)} fusion(f32[512,2048]{0,1:T(8,128)} %get-tuple-element.9, f32[1,512]{1,0:T(1,128)S(1)} %copy-done.4), kind=kOutput, calls=%fused_computation.39 | convolution fusion | flops 12582912 | bytes 4204544 | tf_op jit(solution)/shard_map/dot_general | solution.py:77
  431.2 37.7 %psum.7 = f32[2048]{0:T(1024)S(1)} all-reduce(f32[2048]{0:T(1024)S(1)} %broadcast_multiply_fusion.1), channel_id=1, replica_groups=mesh['chan'=8,'split'=4] {'chan','split'}, use_global_device_ids=true, to_apply=%region_2.5 | all-reduce | flops 2048 | bytes 16384 | tf_op jit(solution)/shard_map/psum | solution.py:78
  (41 shorter events, 19.6 us)
Async XLA Ops:
  7.2 1.6 copy-start
  78.6 4.5 copy-start.1
  78.6 51.9 %all-to-all-start.2 = ((bf16[8,64,2048]{2,1,0:T(8,128)(2,1)}), bf16[8,64,2048]{2,1,0:T(8,128)(2,1)}, u32[]{:S(2)}, u32[]{:S(2)}) async-start(bf16[8,64,2048]{2,1,0:T(8,128)(2,1)} %bitcast.64), calls=%async_computation.2 | async-start | bytes 4194304 | tf_op jit(solution)/shard_map/all_to_all | solution.py:41
  83.1 129.6 %all-gather.6.cloned.1.call-start = ((), (), s32[]{:S(2)}) async-start(), calls=%async_computation.5 | async-start | bytes 10485760 | tf_op jit(solution)/shard_map/all_gather | solution.py:57
  145.4 4.0 copy-start.3
  145.4 4.0 copy-start.5
  145.4 4.0 copy-start.6
  155.1 0.8 copy-start.4
  155.1 117.4 %all-gather.8.cloned.1.call-start = ((), (), s32[]{:S(2)}) async-start(), calls=%async_computation.6 | async-start | bytes 10485760 | tf_op jit(solution)/shard_map/all_gather | solution.py:58
  155.9 176.5 %all-gather.4.cloned.1.call-start = ((), (), s32[]{:S(2)}) async-start(), calls=%async_computation.4 | async-start | bytes 10485760 | tf_op jit(solution)/shard_map/all_gather | solution.py:31
  306.1 54.3 %all-to-all-start.3 = ((bf16[8,64,2048]{2,1,0:T(8,128)(2,1)}), bf16[8,64,2048]{2,1,0:T(8,128)(2,1)}, u32[]{:S(2)}, u32[]{:S(2)}) async-start(bf16[8,64,2048]{2,1,0:T(8,128)(2,1)} %select_convert_fusion), calls=%async_computation.3 | async-start | bytes 4194304 | tf_op jit(solution)/shard_map/all_to_all | solution.py:65
  347.4 18.2 %copy-start.2 = (s32[1,512]{1,0:T(1,128)S(1)}, s32[1,512]{1,0:T(1,128)}, u32[]{:S(2)}) copy-start(s32[1,512]{1,0:T(1,128)} %param.19) | copy-start | bytes 6148
  360.5 53.1 %all-to-all-start = ((f32[512,4,512]{2,0,1:T(8,128)}), f32[512,4,512]{2,0,1:T(8,128)}, u32[]{:S(2)}, u32[]{:S(2)}) async-start(f32[512,4,512]{2,0,1:T(8,128)} %copy.19), calls=%async_computation | async-start | bytes 8388608 | tf_op jit(solution)/shard_map/all_to_all | solution.py:34
Sparse Core Ops, SparseCore 0:
  155.3 57.3 all-gather.5
  214.2 58.2 all-gather.7
  274.1 58.2 all-gather.3
where the time goes:
time: 477 us; the launch traced here: 476 us
  waiting for transfers between devices  191 us (40%)
  local copies, waits for them, and re-layouts  98.4 us (21%)
  blocking collectives  93.1 us (20%)
  matrix products  37.2 us (8%)
  other arithmetic  26.7 us (6%)
  starting transfers between devices  15.3 us (3%)
  between operations  13.9 us (3%)
    all_to_all x1, blocking collectives, on_device(): lax.all_to_all(sorted_o, 'chan', split_axis=0, concat_axis=0, tiled=True)  55.4 us
    all_gather x1, waiting for transfers between devices, on_device(): lax.all_gather(right_o, 'split', axis=0, tiled=True)  49.2 us
    all_gather x1, waiting for transfers between devices, on_device(): lax.all_gather(right_h, 'split', axis=0, tiled=True)  45 us
    psum x1, blocking collectives, on_device(): one_body = lax.psum(local_part, ('chan', 'split')) * norm_factor  37.7 us
    all_to_all x1, waiting for transfers between devices, on_device(): lax.all_to_all(half_rows, 'split', split_axis=1, concat_axis=0, tiled=True)  34.5 us
    all_to_all x1, waiting for transfers between devices, on_device(): lax.all_to_all(sorted_h, 'chan', split_axis=0, concat_axis=0, tiled=True)  28.3 us
    all_gather x1, waiting for transfers between devices, on_device(): lax.all_gather(scaled_h, 'split', axis=0, tiled=True)  20.6 us
    gather x2, local copies, waits for them, and re-layouts, on_device(): bar_o = (coefs * jnp.take(recv_o, perm_cols, axis=1)).astype(jnp.bfloat16)  15.1 us
  transfers between devices with their start and end apart: 6, of which 6 were waited for; matrix products, arithmetic and copies ran while one was open for 22% of the time, Pallas kernels for 0%

commit v1 on v0

v1 whole, which is shorter than its diff:
```python
import math

import jax
import jax.numpy as jnp
from jax import lax
from jax.sharding import PartitionSpec as P

F32, BF16 = jnp.float32, jnp.bfloat16


def dot(a, b):
    return jnp.dot(a, b, preferred_element_type=F32)


def prepare(omega, hamil, pp_sign, ph_sign, row_coef, col_coef, col_perm, send_order):
    chan_count = lax.axis_size("chan")
    _, height, breadth = omega.shape
    slots = height // chan_count
    active = height // 16
    me_c, me_s = lax.axis_index("chan"), lax.axis_index("split")
    sign = ph_sign[0]
    mask = sign != 0
    lower = jnp.arange(height)[:, None] <= jnp.arange(height)[None, :]
    rank = jnp.sum(jnp.where(lower & mask[:, None], 1, 0), axis=0) - 1
    rank = jnp.where(mask, rank, -1)
    pick = rank[None, :] == jnp.arange(active)[:, None]
    own_perm = lax.dynamic_slice(col_perm[0], (me_s * height,), (height,))
    own_cc = lax.dynamic_slice(col_coef[0], (me_s * height,), (height,))

    def picked(values):
        return jnp.sum(jnp.where(pick, values[None, :].astype(F32), 0.0), axis=1)

    pack = jnp.concatenate(
        [picked(own_perm), picked(own_cc), rank.astype(F32), pp_sign[0]]
    )
    packs = lax.all_gather(pack, ("chan", "split"), axis=0, tiled=False)
    packs = packs.reshape(chan_count, -1, pack.shape[0])
    cols = packs[:, :, :active].reshape(chan_count, -1).astype(jnp.int32)
    act_cc = lax.dynamic_index_in_dim(packs, me_c, 0, False)[:, active : 2 * active].reshape(-1)
    ranks = lax.dynamic_index_in_dim(packs, me_s, 1, False)[:, 2 * active : 2 * active + height]
    ranks = lax.dynamic_slice(ranks, (0, me_c * slots), (chan_count, slots)).astype(jnp.int32)
    signs_all = lax.dynamic_index_in_dim(packs, me_c, 0, False)[:, 2 * active + height :]
    hit = col_perm[0][:, None] == jnp.arange(breadth)[None, :]
    cc_inv = jnp.sum(jnp.where(hit, col_coef[0][:, None], 0.0), axis=0)
    order = (send_order[0][:, None] == jnp.arange(height)[None, :]).astype(BF16)
    return dict(
        cols=cols, act_cc=act_cc, ranks=ranks, signs_all=signs_all, cc_inv=cc_inv,
        order=order, act_rc=picked(row_coef[0]), act_sign=picked(sign), active=active,
    )


def on_device(omega, hamil, pp_sign, ph_sign, row_coef, col_coef, col_perm, send_order):
    chan_count = lax.axis_size("chan")
    _, height, breadth = omega.shape
    slots = height // chan_count
    me_c = lax.axis_index("chan")
    pre = prepare(omega, hamil, pp_sign, ph_sign, row_coef, col_coef, col_perm, send_order)
    active, order = pre["active"], pre["order"]
    omega_rows, hamil_rows = omega[0], hamil[0]

    scaled_h = (pp_sign[0][:, None] * hamil_rows).astype(BF16)
    all_h = lax.all_gather(scaled_h, "split", axis=0, tiled=True)

    sorted_o = dot(order, omega_rows).astype(BF16).reshape(chan_count, slots, breadth)
    sorted_h = dot(order, hamil_rows).astype(BF16).reshape(chan_count, slots, breadth)
    take = (pre["ranks"][:, None, :] == jnp.arange(active)[None, :, None]).astype(BF16)
    gate = (pre["cols"][:, None, :] == jnp.arange(breadth)[None, :, None]).astype(BF16)

    def batched(a, b):
        return jnp.einsum("qik,qkj->qij", a, b, preferred_element_type=F32).astype(BF16)

    parts = [batched(take, sorted_o), batched(take, sorted_h)]
    wide = pre["cols"].shape[1]
    left = jnp.concatenate([batched(sorted_o, gate), batched(sorted_h, gate)], axis=1)
    parts.append(left.reshape(chan_count, -1, breadth))
    sent = jnp.concatenate(parts, axis=1)
    got = lax.all_to_all(sent, "chan", split_axis=0, concat_axis=0, tiled=True)
    rows = jnp.sum(got[:, : 2 * active].astype(F32), axis=0)
    lefts = got[:, 2 * active :].reshape(chan_count, 2, slots, wide)
    coef_a = pre["act_rc"][:, None] * pre["cc_inv"][None, :]
    right_o = pre["act_sign"][:, None] * (coef_a * rows[:active]).astype(BF16).astype(F32)
    right_h = pre["act_sign"][:, None] * (coef_a * rows[active:]).astype(BF16).astype(F32)
    right = jnp.stack([right_h, right_o]).astype(BF16)
    rights = lax.all_gather(right, "split", axis=1, tiled=True)
    coef_l = row_coef[0][:, None] * pre["act_cc"][None, :]
    bar_o = (coef_l * lefts[:, 0].reshape(height, wide)).astype(BF16)
    bar_h = (coef_l * lefts[:, 1].reshape(height, wide)).astype(BF16)
    ph_sum = dot(jnp.concatenate([bar_o, -bar_h], axis=1), rights.reshape(-1, breadth))
    coefs = row_coef[0][:, None] * pre["cc_inv"][None, :]
    back = (coefs * ph_sum).astype(BF16)

    half = dot(omega_rows, all_h)
    flipped = lax.all_to_all(half.astype(BF16), "split", split_axis=1, concat_axis=0, tiled=True)

    returned = lax.all_to_all(
        back.reshape(chan_count, slots, breadth), "chan", split_axis=0, concat_axis=0, tiled=True
    )
    placed = lax.dot_general(
        order, returned.reshape(height, breadth), (((0,), (0,)), ((), ())),
        preferred_element_type=F32,
    )
    combined = half + flipped.T.astype(F32) + placed
    degeneracy = (2 * (me_c // 2) + 1).astype(F32)
    weight_sq = sum((2 * (i // 2) + 1) ** 2 for i in range(chan_count))
    local = degeneracy * jnp.sum(pp_sign[0][:, None] * combined, axis=0)
    one_body = lax.psum(local, ("chan", "split")) * (1.0 / math.sqrt(breadth * weight_sq))
    return combined.astype(BF16)[None], one_body


def solution(mesh):
    in_specs = (
        P("chan", "split", None),
        P("chan", "split", None),
        P("chan", "split"),
        P("chan", "split"),
        P("chan", "split"),
        P("chan", None),
        P("chan", None),
        P("chan", "split"),
    )
    out_specs = (P("chan", "split", None), P())
    return jax.shard_map(
        on_device, mesh=mesh, in_specs=in_specs, out_specs=out_specs, check_vma=False
    )
```

time: 477 us -> 394 us (0.83)
  local copies, waits for them, and re-layouts: 98.4 us -> 17.8 us
  waiting for transfers between devices: 191 us -> 251 us
  blocking collectives: 93.1 us -> 37.6 us
  other arithmetic: 26.7 us -> 20.7 us
    unnamed x3 -> x4, waiting for transfers between devices: 0.73 us -> 137 us
    all_gather x3 -> x2, waiting for transfers between devices: 115 us -> 0.05 us  [the longest x1 0.03 us: on_device(): all_h = lax.all_gather(scaled_h, 'split', axis=0, tiled=True)]
    gather x10 -> x0, local copies, waits for them, and re-layouts: 66.5 us -> none  [the longest x2 15.1 us: on_device(): bar_o = (coefs * jnp.take(recv_o, perm_cols, axis=1)).astype(jnp.bfloat16)]
    all_to_all x1 -> x0, blocking collectives: 55.4 us -> none  [on_device(): lax.all_to_all(sorted_o, 'chan', split_axis=0, concat_axis=0, tiled=True)]
    all_to_all x3, waiting for transfers between devices: 75.8 us -> 114 us  [the longest x1 50.4 us: on_device(): got = lax.all_to_all(sent, 'chan', split_axis=0, concat_axis=0, tiled=True)]
    scatter x2 -> x0, local copies, waits for them, and re-layouts: 10.7 us -> none  [the longest x1 8.23 us: on_device(): jnp.zeros((breadth,), jnp.int32).at[perm_cols]]
    broadcast_in_dim x1 -> x0, other arithmetic: 7.97 us -> none  [on_device(): return (combined.astype(jnp.bfloat16)[None], one_body)]
    convert_element_type x3 -> x6, other arithmetic: 12.6 us -> 4.98 us  [the longest x1 3.38 us: on_device(): scaled_h = (pp_sign[0][:, None] * hamil_rows).astype(BF16)]
  transfers between devices with their start and end apart: 6 -> 6, of which waited for: 6 -> 4; matrix products, arithmetic and copies ran while one was open for 22% -> 14% of each run, Pallas kernels for 0% -> 0%
where the time goes in v1:
time: 394 us; the launch traced here: 393 us
  waiting for transfers between devices  251 us (64%)
  blocking collectives  37.6 us (10%)
  matrix products  33.6 us (9%)
  other arithmetic  20.7 us (5%)
  local copies, waits for them, and re-layouts  17.8 us (5%)
  starting transfers between devices  16.3 us (4%)
  between operations  15.7 us (4%)
    unnamed x4, waiting for transfers between devices  137 us
    all_to_all x1, waiting for transfers between devices, on_device(): got = lax.all_to_all(sent, 'chan', split_axis=0, concat_axis=0, tiled=True)  50.4 us
    all_to_all x1, waiting for transfers between devices, on_device(): lax.all_to_all(back.reshape(chan_count, slots, breadth), 'chan', split_ax...  42.7 us
    psum x1, blocking collectives, on_device(): lax.psum(local, ('chan', 'split')) * (1.0 / math.sqrt(breadth * weight_sq))  37.6 us
    all_to_all x1, waiting for transfers between devices, on_device(): lax.all_to_all(half.astype(BF16), 'split', split_axis=1, concat_axis=0, t...  20.9 us
    dot_general x4, matrix products, dot(): return jnp.dot(a, b, preferred_element_type=F32)  20 us
    unnamed x23, local copies, waits for them, and re-layouts  9.53 us
    dot_general x4, matrix products, batched(): jnp.einsum('qik,qkj->qij', a, b, preferred_element_type=F32).astype(BF16)  7.9 us
  transfers between devices with their start and end apart: 6, of which 4 were waited for; matrix products, arithmetic and copies ran while one was open for 14% of the time, Pallas kernels for 0%

profile of v1, /device:TPU:0, one launch (start us, length us, event | category | flops | bytes accessed | tf_op | source)
XLA Modules:
  0.0 393.0 jit_solution(4164842909962575197)
XLA Ops:
  8.1 0.8 broadcast_compare_fusion
  9.0 0.7 constant_dynamic-slice_fusion.1
  10.4 0.7 select_convert_fusion
  11.8 0.9 select_reduce_fusion.3
  12.6 0.8 concatenate.12
  14.5 3.9 copy.14
  18.4 3.4 multiply_convert_fusion.1
  22.5 4.2 %convolution_convert_fusion = bf16[512,2048]{1,0:T(8,128)(2,1)} fusion(bf16[1,512,2048]{2,1,0:T(8,128)(2,1)} %param.9, s32[512]{0:T(512)S(1)} %bitcast.86), kind=kOutput, calls=%fused_computation.13 | convolution fusion | flops 1075052544 | bytes 4196352 | tf_op jit(solution)/shard_map/dot_general | solution.py:12
  26.7 2.6 convolution_convert_fusion.1
  29.4 137.1 %all-reduce.3.cloned.1.call-done = f32[34816]{0:T(1024)} async-done(((f32[34816]{0:T(1024)}), f32[34816]{0:T(1024)}) %all-reduce.3.cloned.1.call-update) | async-done | bytes 139280
  166.5 1.1 reshape.74
  167.7 3.5 fusion.9
  171.3 1.8 fusion.8
  173.3 2.1 convolution_convert_fusion.2
  175.9 1.6 pad_maximum_fusion
  177.5 7.1 %all-to-all-start.1 = ((bf16[8,72,2048]{2,1,0:T(8,128)(2,1)}), bf16[8,72,2048]{2,1,0:T(8,128)(2,1)}, u32[]{:S(2)}, u32[]{:S(2)}) async-start(bf16[8,72,2048]{2,1,0:T(8,128)(2,1)} %pad_maximum_fusion), calls=%async_computation.1 | async-start | bytes 4718592 | tf_op jit(solution)/shard_map/all_to_all | solution.py:77
  184.8 2.4 select_reduce_fusion
  187.3 50.4 %all-to-all-done.1 = bf16[8,72,2048]{2,1,0:T(8,128)(2,1)} async-done(((bf16[8,72,2048]{2,1,0:T(8,128)(2,1)}), bf16[8,72,2048]{2,1,0:T(8,128)(2,1)}, u32[]{:S(2)}, u32[]{:S(2)}) %all-to-all-start.1) | async-done | bytes 2359328 | tf_op jit(solution)/shard_map/all_to_all | solution.py:77
  237.7 2.0 convert_reduce_fusion
  239.8 0.7 pad_maximum_fusion.2
  240.6 9.9 %fusion.28 = (bf16[2048,512]{1,0:T(8,128)(2,1)}, f32[2048,512]{1,0:T(8,128)}) fusion(bf16[2048,2048]{0,1:T(8,128)(2,1)} %all-gather.4.cloned.1.call-done, bf16[1,512,2048]{2,1,0:T(8,128)(2,1)S(1)} %copy-done), kind=kOutput, calls=%fused_computation.73 | convolution fusion | flops 4296015872 | bytes 16777216 | tf_op jit(solution)/shard_map/dot_general | solution.py:12
  250.5 4.2 %copy.15 = bf16[512,4,512]{2,0,1:T(8,128)(2,1)} copy(bf16[512,4,512]{0,2,1:T(8,128)(2,1)} %bitcast.67) | data formatting | bytes 4194304 | tf_op jit(solution)/shard_map/all_to_all | solution.py:93
  254.6 4.6 %all-to-all-start = ((bf16[512,4,512]{2,0,1:T(8,128)(2,1)}), bf16[512,4,512]{2,0,1:T(8,128)(2,1)}, u32[]{:S(2)}, u32[]{:S(2)}) async-start(bf16[512,4,512]{2,0,1:T(8,128)(2,1)} %copy.15), calls=%async_computation | async-start | bytes 4194304 | tf_op jit(solution)/shard_map/all_to_all | solution.py:93
  259.4 1.0 slice.39
  260.9 3.3 multiply_convert_fusion
  264.1 20.9 %all-to-all-done = bf16[512,4,512]{2,0,1:T(8,128)(2,1)} async-done(((bf16[512,4,512]{2,0,1:T(8,128)(2,1)}), bf16[512,4,512]{2,0,1:T(8,128)(2,1)}, u32[]{:S(2)}, u32[]{:S(2)}) %all-to-all-start) | async-done | bytes 2097184 | tf_op jit(solution)/shard_map/all_to_all | solution.py:93
  285.0 4.4 %all-to-all-start.2 = ((bf16[8,64,2048]{2,1,0:T(8,128)(2,1)}), bf16[8,64,2048]{2,1,0:T(8,128)(2,1)}, u32[]{:S(2)}, u32[]{:S(2)}) async-start(bf16[8,64,2048]{2,1,0:T(8,128)(2,1)} %bitcast.66), calls=%async_computation.2 | async-start | bytes 4194304 | tf_op jit(solution)/shard_map/all_to_all | solution.py:95
  289.4 5.6 %bitcast_add_fusion = f32[2048,512]{1,0:T(8,128)} fusion(f32[2048,512]{1,0:T(8,128)} %get-tuple-element.19, bf16[512,4,512]{2,0,1:T(8,128)(2,1)} %all-to-all-done), kind=kLoop, calls=%fused_computation.5 | loop fusion | flops 2097152 | bytes 10485760 | tf_op jit(solution)/shard_map/add | solution.py:102
  294.9 42.7 %all-to-all-done.2 = bf16[8,64,2048]{2,1,0:T(8,128)(2,1)} async-done(((bf16[8,64,2048]{2,1,0:T(8,128)(2,1)}), bf16[8,64,2048]{2,1,0:T(8,128)(2,1)}, u32[]{:S(2)}, u32[]{:S(2)}) %all-to-all-start.2) | async-done | bytes 2097184 | tf_op jit(solution)/shard_map/all_to_all | solution.py:95
  337.7 5.7 %multiply_reduce_fusion = (f32[2048]{0:T(1024)S(1)}, bf16[1,512,2048]{1,2,0:T(8,128)(2,1)}) fusion(f32[512]{0:T(512)S(1)} %bitcast.78, bf16[512,2048]{1,0:T(8,128)(2,1)} %bitcast.26, s32[512]{0:T(512)S(1)} %bitcast.88, f32[2048,512]{1,0:T(8,128)} %bitcast_add_fusion), kind=kOutput, calls=%fused_computation.7 | convolution fusion | flops 1078196224 | bytes 8400896 | tf_op jit(solution)/shard_map/dot_general | solution.py:98
  343.4 37.6 %psum.7 = f32[2048]{0:T(1024)S(1)} all-reduce(f32[2048]{0:T(1024)S(1)} %broadcast_multiply_fusion.1), channel_id=1, replica_groups=mesh['chan'=8,'split'=4] {'chan','split'}, use_global_device_ids=true, to_apply=%region_8.9 | all-reduce | flops 2048 | bytes 16384 | tf_op jit(solution)/shard_map/psum | solution.py:106
  381.6 3.9 copy.17
  (50 shorter events, 5.8 us)
Async XLA Ops:
  8.0 18.7 %copy-start = (bf16[1,512,2048]{2,1,0:T(8,128)(2,1)S(1)}, bf16[1,512,2048]{2,1,0:T(8,128)(2,1)}, u32[]{:S(2)}) copy-start(bf16[1,512,2048]{2,1,0:T(8,128)(2,1)} %param.8) | copy-start | bytes 6291460
  8.0 158.4 %all-reduce.3.cloned.1.call-start = ((), (), s32[]{:S(2)}) async-start(), calls=%async_computation.5 | async-start | bytes 278528
  13.8 0.7 copy-start.3
  14.4 4.0 %copy-start.5 = (f32[1,512]{1,0:T(1,128)S(1)}, f32[1,512]{1,0:T(1,128)}, u32[]{:S(2)}) copy-start(f32[1,512]{1,0:T(1,128)} %param.10) | copy-start | bytes 6148
  14.5 226.1 %all-gather.4.cloned.1.call-start = ((), (), s32[]{:S(2)}) async-start(), calls=%async_computation.3 | async-start | bytes 10485760 | tf_op jit(solution)/shard_map/all_gather | solution.py:62
  21.8 0.7 copy-start.8
  167.7 3.5 copy-start.1
  173.2 2.2 copy-start.2
  177.5 7.3 %copy-start.6 = (f32[1,2048]{1,0:T(1,128)S(1)}, f32[1,2048]{1,0:T(1,128)}, u32[]{:S(2)}) copy-start(f32[1,2048]{1,0:T(1,128)} %param.13) | copy-start | bytes 24580
  177.5 7.3 %copy-start.7 = (s32[1,2048]{1,0:T(1,128)S(1)}, s32[1,2048]{1,0:T(1,128)}, u32[]{:S(2)}) copy-start(s32[1,2048]{1,0:T(1,128)} %param.14) | copy-start | bytes 24580
  177.5 60.2 %all-to-all-start.1 = ((bf16[8,72,2048]{2,1,0:T(8,128)(2,1)}), bf16[8,72,2048]{2,1,0:T(8,128)(2,1)}, u32[]{:S(2)}, u32[]{:S(2)}) async-start(bf16[8,72,2048]{2,1,0:T(8,128)(2,1)} %pad_maximum_fusion), calls=%async_computation.1 | async-start | bytes 4718592 | tf_op jit(solution)/shard_map/all_to_all | solution.py:77
  184.6 76.3 %all-gather.6.cloned.1.call-start = ((), (), s32[]{:S(2)}) async-start(), calls=%async_computation.4 | async-start | bytes 1310720 | tf_op jit(solution)/shard_map/all_gather | solution.py:84
  254.6 5.9 %copy-start.4 = (f32[1,512]{1,0:T(1,128)S(1)}, f32[1,512]{1,0:T(1,128)}, u32[]{:S(2)}) copy-start(f32[1,512]{1,0:T(1,128)} %param.12) | copy-start | bytes 6148
  254.6 30.3 %all-to-all-start = ((bf16[512,4,512]{2,0,1:T(8,128)(2,1)}), bf16[512,4,512]{2,0,1:T(8,128)(2,1)}, u32[]{:S(2)}, u32[]{:S(2)}) async-start(bf16[512,4,512]{2,0,1:T(8,128)(2,1)} %copy.15), calls=%async_computation | async-start | bytes 4194304 | tf_op jit(solution)/shard_map/all_to_all | solution.py:93
  285.0 52.7 %all-to-all-start.2 = ((bf16[8,64,2048]{2,1,0:T(8,128)(2,1)}), bf16[8,64,2048]{2,1,0:T(8,128)(2,1)}, u32[]{:S(2)}, u32[]{:S(2)}) async-start(bf16[8,64,2048]{2,1,0:T(8,128)(2,1)} %bitcast.66), calls=%async_computation.2 | async-start | bytes 4194304 | tf_op jit(solution)/shard_map/all_to_all | solution.py:95
Sparse Core Ops, SparseCore 0:
  14.6 151.8 all-reduce.2
Sparse Core Ops, SparseCore 1:
  21.9 61.0 all-gather.3
  240.7 15.5 all-gather.5

commit v2 on v1

--- a/solution.py
+++ b/solution.py
@@ -1,8 +1,11 @@
+import functools
 import math
 
 import jax
 import jax.numpy as jnp
 from jax import lax
+from jax.experimental import pallas as pl
+from jax.experimental.pallas import tpu as pltpu
 from jax.sharding import PartitionSpec as P
 
 F32, BF16 = jnp.float32, jnp.bfloat16
@@ -107,7 +110,325 @@
     return combined.astype(BF16)[None], one_body
 
 
+NT = (((1,), (1,)), ((), ()))
+
+
+def fused(norm, omega, hamil, meta, ranks, cc_inv, colvec, actvec, order, order_t,
+          z_out, ob_out,
+          part_o, part_h, scal_o, scal_h, meta1, meta2s, meta2, sorted_r,
+          send_a, recv_a, send_l, recv_l, ladder, x_send, x_recv, acc, rights,
+          bars, back_s, back_r, ob1, ob2, right_s,
+          p_send, p_recv, m1_send, m1_recv, m2_send, m2_recv, a_send, a_recv,
+          l_send, l_recv, x_ss, x_rs, r_send, r_recv, b_send, b_recv,
+          o1_send, o1_recv, o2_send, o2_recv):
+    chans, splits = ob2.shape[0], ob1.shape[0]
+    height, breadth = omega.shape
+    slots = height // chans
+    active = height // 16
+    wide = active * splits
+    c, s = lax.axis_index("chan"), lax.axis_index("split")
+    partner = s + 1 - 2 * lax.rem(s, 2)
+    far = 2 * (1 - s // 2)
+    MESH = pl.DeviceIdType.MESH
+
+    def remote(src, dst, ss, rs, cc, sp):
+        return pltpu.make_async_remote_copy(
+            src_ref=src, dst_ref=dst, send_sem=ss, recv_sem=rs,
+            device_id=(cc, sp), device_id_type=MESH)
+
+    def chan_loop(body):
+        def step(d, carry):
+            body(lax.rem(c + 1 + d, chans))
+            return carry
+        lax.fori_loop(0, chans - 1, step, 0)
+
+    def split_loop(body):
+        def step(d, carry):
+            body(lax.rem(s + 1 + d, splits))
+            return carry
+        lax.fori_loop(0, splits - 1, step, 0)
+
+    barrier = pltpu.get_barrier_semaphore()
+
+    def greet(cc, sp):
+        pl.semaphore_signal(barrier, inc=1, device_id=(cc, sp), device_id_type=MESH)
+
+    chan_loop(lambda q: greet(q, s))
+    split_loop(lambda p: greet(c, p))
+    pl.semaphore_wait(barrier, chans + splits - 2)
+
+    def m1(p, frm):
+        return remote(meta, meta1.at[frm], m1_send.at[p], m1_recv.at[frm], c, p)
+    split_loop(lambda p: m1(p, s).start())
+    meta1[s] = meta[...]
+
+    copy_o = remote(omega, part_o, p_send.at[0], p_recv.at[0], c, partner)
+    copy_h = remote(hamil, part_h, p_send.at[1], p_recv.at[1], c, partner)
+    copy_o.start()
+    copy_h.start()
+
+    tile = 256
+    def sort_tile(n, carry):
+        cols = pl.ds(pl.multiple_of(n * tile, tile), tile)
+        got = dot(order[...], omega[:, cols]).astype(BF16)
+        sorted_r[:, :slots, cols] = got.reshape(chans, slots, tile)
+        got = dot(order[...], hamil[:, cols]).astype(BF16)
+        sorted_r[:, slots:, cols] = got.reshape(chans, slots, tile)
+        return carry
+    lax.fori_loop(0, breadth // tile, sort_tile, 0)
+
+    split_loop(lambda p: m1(p, p).wait_recv())
+    sums = meta1[0] + meta1[1] + meta1[2] + meta1[3]
+    cols_row, act_cc = sums[0:1, :wide], sums[1:2, :wide]
+    for q in range(chans):
+        meta2s[q] = ranks[q]
+        meta2s[q, 0:1, :] = cols_row
+
+    def m2(q, frm):
+        return remote(meta2s.at[q], meta2.at[frm], m2_send.at[q], m2_recv.at[frm], q, s)
+    chan_loop(lambda q: m2(q, c).start())
+    meta2[c] = meta2s[c]
+
+    def copy_a(q, frm):
+        return remote(send_a.at[q], recv_a.at[frm], a_send.at[q], a_recv.at[frm], q, s)
+
+    def copy_l(q, frm):
+        return remote(send_l.at[q], recv_l.at[frm], l_send.at[q], l_recv.at[frm], q, s)
+
+    def pack(q, rows_to, left_to):
+        want = meta2[q]
+        take = lax.broadcasted_iota(jnp.int32, (active, slots), 0).astype(F32)
+        take = jnp.where(take == want[1:2, :slots], 1.0, 0.0).astype(BF16)
+        rows_to[q, :active] = dot(take, sorted_r[q, :slots]).astype(BF16)
+        rows_to[q, active:] = dot(take, sorted_r[q, slots:]).astype(BF16)
+        gate = lax.broadcasted_iota(jnp.int32, (breadth, wide), 0).astype(F32)
+        gate = jnp.where(gate == want[0:1, :wide], 1.0, 0.0).astype(BF16)
+        left_to[q] = dot(sorted_r[q], gate).astype(BF16)
+
+    def pack_send(q):
+        m2(q, q).wait_recv()
+        pack(q, send_a, send_l)
+        copy_a(q, c).start()
+        copy_l(q, c).start()
+    chan_loop(pack_send)
+    pack(c, recv_a, recv_l)
+
+    span = height
+    for k in range(splits):
+        cols = slice(k * span, (k + 1) * span)
+        sgn = meta1[k, 2:3, :]
+        scal_o[:, cols] = (omega[:, cols].astype(F32) * sgn).astype(BF16)
+        scal_h[:, cols] = (hamil[:, cols].astype(F32) * sgn).astype(BF16)
+    copy_o.wait_recv()
+    copy_h.wait_recv()
+    own = pl.ds(pl.multiple_of(s * span, span), span)
+    oth = pl.ds(pl.multiple_of(partner * span, span), span)
+
+    def cross(m, carry):
+        def half_tile(t, carry):
+            cols = pl.ds(pl.multiple_of((far + m) * span + t * tile, tile), tile)
+            val = dot(scal_o[:, own], hamil[:, cols]) - dot(scal_h[:, own], omega[:, cols])
+            val = val + dot(scal_o[:, oth], part_h[:, cols]) - dot(scal_h[:, oth], part_o[:, cols])
+            ladder[:, cols] = val
+            x_send[m, :, pl.ds(pl.multiple_of(t * tile, tile), tile)] = val.astype(BF16)
+            return carry
+        return lax.fori_loop(0, span // tile, half_tile, carry)
+
+    def copy_x(m, frm):
+        return remote(x_send.at[m], x_recv.at[frm], x_ss.at[m], x_rs.at[frm], c, far + m)
+    core = lax.rem(s, 2)
+    for m in range(2):
+        cross(m, 0)
+        copy_x(m, core).start()
+
+    def same(t, carry):
+        rows = pl.ds(pl.multiple_of(t * tile, tile), tile)
+        val = lax.dot_general(scal_o[...], part_h[rows], NT, preferred_element_type=F32)
+        val = val + lax.dot_general(scal_h[...], part_o[rows], NT, preferred_element_type=F32)
+        ladder[:, pl.ds(pl.multiple_of(partner * span + t * tile, tile), tile)] = val
+        val = lax.dot_general(scal_o[...], hamil[rows], NT, preferred_element_type=F32)
+        val = val + lax.dot_general(scal_h[...], omega[rows], NT, preferred_element_type=F32)
+        ladder[:, pl.ds(pl.multiple_of(s * span + t * tile, tile), tile)] = val
+        return carry
+    lax.fori_loop(0, span // tile, same, 0)
+
+    acc[...] = recv_a[c].astype(F32)
+
+    def add_rows(q):
+        copy_a(q, q).wait_recv()
+        acc[...] += recv_a[q].astype(F32)
+    chan_loop(add_rows)
+    coef_a = actvec[:, 0:1] * cc_inv[...]
+    signs = actvec[:, 1:2]
+    right_s[1] = (-signs * (coef_a * acc[:active]).astype(BF16).astype(F32)).astype(BF16)
+    right_s[0] = (signs * (coef_a * acc[active:]).astype(BF16).astype(F32)).astype(BF16)
+
+    def place(p):
+        return rights.at[:, pl.ds(pl.multiple_of(p * active, active), active), :]
+
+    def copy_r(p, frm):
+        return remote(right_s, place(frm), r_send.at[p], r_recv.at[frm], c, p)
+    split_loop(lambda p: copy_r(p, s).start())
+    rights[:, pl.ds(pl.multiple_of(s * active, active), active), :] = right_s[...]
+
+    def make_bars(q):
+        rows = pl.ds(pl.multiple_of(q * slots, slots), slots)
+        coef = colvec[rows, 1:2] * act_cc
+        bars[rows, :wide] = (coef * recv_l[q, :slots].astype(F32)).astype(BF16)
+        bars[rows, wide:] = (coef * recv_l[q, slots:].astype(F32)).astype(BF16)
+
+    def bars_from(q):
+        copy_l(q, q).wait_recv()
+        make_bars(q)
+    chan_loop(bars_from)
+    make_bars(c)
+    split_loop(lambda p: copy_r(p, p).wait_recv())
+
+    def copy_b(q, frm):
+        return remote(back_s.at[q], back_r.at[frm], b_send.at[q], b_recv.at[frm], q, s)
+
+    def product(q, to):
+        rows = pl.ds(pl.multiple_of(q * slots, slots), slots)
+        val = dot(bars[rows, :wide], rights[0]) + dot(bars[rows, wide:], rights[1])
+        to[q] = (colvec[rows, 1:2] * cc_inv[...] * val).astype(BF16)
+
+    def product_send(q):
+        product(q, back_s)
+        copy_b(q, c).start()
+    chan_loop(product_send)
+    product(c, back_r)
+
+    for m in range(2):
+        copy_x(m, m).wait_recv()
+        def flip(t, carry):
+            val = x_recv[m, :, pl.ds(pl.multiple_of(t * tile, tile), tile)]
+            cols = pl.ds(pl.multiple_of((far + m) * span, span), span)
+            ladder[pl.ds(pl.multiple_of(t * tile, tile), tile), cols] += val.astype(F32).T
+            return carry
+        lax.fori_loop(0, span // tile, flip, 0)
+
+    chan_loop(lambda q: copy_b(q, q).wait_recv())
+
+    degeneracy = (2 * (c // 2) + 1).astype(F32)
+    weight = degeneracy * colvec[:, 0:1]
+
+    def finish(n, carry):
+        cols = pl.ds(pl.multiple_of(n * tile, tile), tile)
+        total = ladder[:, cols] + dot(order_t[...], back_r[:, :, cols].reshape(height, tile))
+        z_out[:, cols] = total.astype(BF16)
+        ob1[s, pl.ds(n, 1), :] = jnp.sum(weight * total, axis=0, keepdims=True)
+        return carry
+    lax.fori_loop(0, breadth // tile, finish, 0)
+
+    def copy_o1(p, frm):
+        return remote(ob1.at[s], ob1.at[frm], o1_send.at[p], o1_recv.at[frm], c, p)
+    split_loop(lambda p: copy_o1(p, s).start())
+    split_loop(lambda p: copy_o1(p, p).wait_recv())
+    ob2[c] = ob1[0] + ob1[1] + ob1[2] + ob1[3]
+
+    def copy_o2(q, frm):
+        return remote(ob2.at[c], ob2.at[frm], o2_send.at[q], o2_recv.at[frm], q, s)
+    chan_loop(lambda q: copy_o2(q, c).start())
+    chan_loop(lambda q: copy_o2(q, q).wait_recv())
+    whole = ob2[0]
+    for q in range(1, chans):
+        whole = whole + ob2[q]
+    ob_out[...] = whole * norm
+
+    split_loop(lambda p: m1(p, s).wait_send())
+    split_loop(lambda p: copy_r(p, s).wait_send())
+    split_loop(lambda p: copy_o1(p, s).wait_send())
+    copy_o.wait_send()
+    copy_h.wait_send()
+    for m in range(2):
+        copy_x(m, core).wait_send()
+
+    def sent(q):
+        m2(q, c).wait_send()
+        copy_a(q, c).wait_send()
+        copy_l(q, c).wait_send()
+        copy_b(q, c).wait_send()
+        copy_o2(q, c).wait_send()
+    chan_loop(sent)
+
+
+def on_device_fused(omega, hamil, pp_sign, ph_sign, row_coef, col_coef, col_perm, send_order):
+    chans, splits = lax.axis_size("chan"), lax.axis_size("split")
+    _, height, breadth = omega.shape
+    slots, active = height // chans, height // 16
+    wide = active * splits
+    me_s = lax.axis_index("split")
+    sign = ph_sign[0]
+    mask = sign != 0
+    lower = jnp.arange(height)[:, None] <= jnp.arange(height)[None, :]
+    rank = jnp.sum(jnp.where(lower & mask[:, None], 1, 0), axis=0) - 1
+    rank = jnp.where(mask, rank, -1)
+    own_perm = lax.dynamic_slice(col_perm[0], (me_s * height,), (height,)).astype(F32)
+    own_cc = lax.dynamic_slice(col_coef[0], (me_s * height,), (height,))
+    lanes = jnp.arange(height)
+    pick = (rank[:, None] + me_s * active == lanes[None, :]) & mask[:, None]
+
+    def picked(values):
+        return jnp.sum(jnp.where(pick, values[:, None], 0.0), axis=0)
+    pad = jnp.zeros((5, height), F32)
+    meta = jnp.concatenate(
+        [picked(own_perm)[None], picked(own_cc)[None], pp_sign[0][None], pad])
+    ranks = jnp.pad(rank.astype(F32).reshape(chans, 1, slots),
+                    ((0, 0), (1, 6), (0, wide - slots)), constant_values=-1.0)
+    hit = col_perm[0][:, None] == jnp.arange(breadth)[None, :]
+    cc_inv = jnp.sum(jnp.where(hit, col_coef[0][:, None], 0.0), axis=0)[None]
+    colvec = jnp.stack([pp_sign[0], row_coef[0]], axis=1)
+    colvec = jnp.pad(colvec, ((0, 0), (0, 126)))
+    pick_a = rank[None, :] == jnp.arange(active)[:, None]
+    actvec = jnp.stack([jnp.sum(jnp.where(pick_a, v[None, :], 0.0), axis=1)
+                        for v in (row_coef[0], sign)], axis=1)
+    actvec = jnp.pad(actvec, ((0, 0), (0, 126)))
+    order = (send_order[0][:, None] == lanes[None, :]).astype(BF16)
+    order_t = (send_order[0][None, :] == lanes[:, None]).astype(BF16)
+    weight_sq = sum((2 * (i // 2) + 1) ** 2 for i in range(chans))
+    norm = 1.0 / math.sqrt(breadth * weight_sq)
+    vm = pl.BlockSpec(memory_space=pltpu.VMEM)
+    dma = pltpu.SemaphoreType.DMA
+    z_out, one_body = pl.pallas_call(
+        functools.partial(fused, norm),
+        out_shape=(jax.ShapeDtypeStruct((height, breadth), BF16),
+                   jax.ShapeDtypeStruct((8, breadth // 8), F32)),
+        in_specs=[vm] * 9,
+        out_specs=(vm, vm),
+        scratch_shapes=[
+            pltpu.VMEM((height, breadth), BF16), pltpu.VMEM((height, breadth), BF16),
+            pltpu.VMEM((height, breadth), BF16), pltpu.VMEM((height, breadth), BF16),
+            pltpu.VMEM((splits, 8, height), F32),
+            pltpu.VMEM((chans, 8, wide), F32), pltpu.VMEM((chans, 8, wide), F32),
+            pltpu.VMEM((chans, 2 * slots, breadth), BF16),
+            pltpu.VMEM((chans, 2 * active, breadth), BF16),
+            pltpu.VMEM((chans, 2 * active, breadth), BF16),
+            pltpu.VMEM((chans, 2 * slots, wide), BF16),
+            pltpu.VMEM((chans, 2 * slots, wide), BF16),
+            pltpu.VMEM((height, breadth), F32),
+            pltpu.VMEM((2, height, height), BF16), pltpu.VMEM((2, height, height), BF16),
+            pltpu.VMEM((2 * active, breadth), F32),
+            pltpu.VMEM((2, wide, breadth), BF16),
+            pltpu.VMEM((height, 2 * wide), BF16),
+            pltpu.VMEM((chans, slots, breadth), BF16),
+            pltpu.VMEM((chans, slots, breadth), BF16),
+            pltpu.VMEM((splits, 8, breadth // 8), F32),
+            pltpu.VMEM((chans, 8, breadth // 8), F32),
+            pltpu.VMEM((2, active, breadth), BF16),
+            dma((2,)), dma((2,)), dma((splits,)), dma((splits,)),
+            dma((chans,)), dma((chans,)), dma((chans,)), dma((chans,)),
+            dma((chans,)), dma((chans,)), dma((2,)), dma((2,)),
+            dma((splits,)), dma((splits,)), dma((chans,)), dma((chans,)),
+            dma((splits,)), dma((splits,)), dma((chans,)), dma((chans,)),
+        ],
+        compiler_params=pltpu.CompilerParams(
+            collective_id=0, has_side_effects=True, vmem_limit_bytes=58 * 2**20),
+    )(omega[0], hamil[0], meta, ranks, cc_inv, colvec, actvec, order, order_t)
+    return z_out[None], one_body.reshape(-1)
+
+
 def solution(mesh):
+    small = mesh.shape["chan"] == 8 and mesh.shape["split"] == 4
     in_specs = (
         P("chan", "split", None),
         P("chan", "split", None),
@@ -120,5 +441,5 @@
     )
     out_specs = (P("chan", "split", None), P())
     return jax.shard_map(
-        on_device, mesh=mesh, in_specs=in_specs, out_specs=out_specs, check_vma=False
-    )
+        on_device_fused if small else on_device, mesh=mesh, in_specs=in_specs, out_specs=out_specs, check_vma=False
+    )

time: 394 us -> 159 us (0.40)
  waiting for transfers between devices: 251 us -> 0 us
  Pallas kernels: 0 us -> 138 us
  blocking collectives: 37.6 us -> 0 us
  matrix products: 33.6 us -> 0 us
  starting transfers between devices: 16.3 us -> 0 us
  between operations: 15.7 us -> 0.67 us
  local copies, waits for them, and re-layouts: 17.8 us -> 7.56 us
  other arithmetic: 20.7 us -> 12.6 us
    pallas_call x0 -> x1, Pallas kernels: none -> 138 us  [on_device_fused(): pl.pallas_call(functools.partial(fused, norm), out_shape=(jax.ShapeDtypeS...]
    unnamed x4 -> x0, waiting for transfers between devices: 137 us -> none
    all_to_all x3 -> x0, waiting for transfers between devices: 114 us -> none  [the longest x1 50.4 us: on_device(): got = lax.all_to_all(sent, 'chan', split_axis=0, concat_axis=0, tiled=True)]
    psum x1 -> x0, blocking collectives: 37.6 us -> none  [on_device(): lax.psum(local, ('chan', 'split')) * (1.0 / math.sqrt(breadth * weight_sq))]
    dot_general x9 -> x0, matrix products: 33.6 us -> none  [the longest x4 20 us: dot(): return jnp.dot(a, b, preferred_element_type=F32)]
    all_to_all x3 -> x0, starting transfers between devices: 16 us -> none  [the longest x1 7.09 us: on_device(): got = lax.all_to_all(sent, 'chan', split_axis=0, concat_axis=0, tiled=True)]
    add x1 -> x0, other arithmetic: 5.56 us -> none  [on_device(): combined = half + flipped.T.astype(F32) + placed]
    unnamed x23 -> x2, local copies, waits for them, and re-layouts: 9.53 us -> 4.46 us
  transfers between devices with their start and end apart: 6 -> 0, of which waited for: 4 -> 0; matrix products, arithmetic and copies ran while one was open for 14% -> 0% of each run, Pallas kernels for 0% -> 0%
where the time goes in v2:
time: 159 us
  Pallas kernels  138 us (87%)
  other arithmetic  12.6 us (8%)
  local copies, waits for them, and re-layouts  7.56 us (5%)
    pallas_call x1, Pallas kernels, on_device_fused(): pl.pallas_call(functools.partial(fused, norm), out_shape=(jax.ShapeDtypeS...  138 us
    unnamed x2, local copies, waits for them, and re-layouts  4.46 us
    reduce_sum x1, other arithmetic, on_device_fused(): cc_inv = jnp.sum(jnp.where(hit, col_coef[0][:, None], 0.0), axis=0)[None]  3.86 us

profile of v2, /device:TPU:0, one launch (start us, length us, event | category | flops | bytes accessed | tf_op | source)
XLA Modules:
  0.0 158.8 jit_solution(11653368719394759314)
XLA Ops:
  0.6 0.7 broadcast_compare_fusion
  1.3 0.7 compare_reduce_fusion
  2.0 0.1 pad.22.clone
  2.1 0.2 select_reduce_fusion.3
  2.3 0.7 broadcast_add_fusion
  2.9 0.7 compare_select_fusion
  3.6 0.8 select_reduce_fusion.5
  4.5 0.7 constant_dynamic-slice_fusion
  5.2 0.7 dynamic-slice_convert_fusion
  5.8 0.4 select_reduce_fusion.2
  6.2 0.1 ne.33
  6.3 0.1 sub.9
  6.4 0.7 pad_maximum_fusion
  7.1 3.9 %select_reduce_fusion = f32[2048]{0:T(1024)} fusion(f32[2048]{0:T(1024)} %bitcast.43, s32[2048]{0:T(1024)} %bitcast.42), kind=kLoop, calls=%fused_computation | loop fusion | flops 12580864 | bytes 24576 | tf_op jit(solution)/shard_map/reduce_sum | solution.py:379
  10.9 1.4 maximum_maximum_fusion.meta
  12.3 0.1 copy.22
  12.4 0.6 pad.14.actvec
  13.0 0.6 pad.12.ranks
  13.6 0.1 copy.21
  13.8 0.7 pad.13.colvec
  14.5 1.9 %fusion.3 = (bf16[512,512]{1,0:T(8,128)(2,1)}, bf16[512,512]{1,0:T(8,128)(2,1)}) fusion(s32[512]{0:T(512)} %bitcast.29), kind=kLoop, calls=%fused_computation.12 | loop fusion | flops 1048576 | bytes 1050624 | tf_op jit(solution)/shard_map/convert_element_type | solution.py:387
  16.4 138.0 %shard_map.95 = (bf16[512,2048]{1,0:T(8,128)(2,1)}, f32[8,256]{1,0:T(8,128)}) custom-call(bf16[512,2048]{1,0:T(8,128)(2,1)} %bitcast.21, bf16[512,2048]{1,0:T(8,128)(2,1)} %bitcast.22, f32[8,512]{1,0:T(8,128)} %maximum_maximum_fusion.meta, f32[8,8,128]{2,1,0:T(8,128)} %pad.12.ranks, f32[1,2048]{1,0:T(1,128)} %bitcast.28, f32[512,128]{1,0:T(8,128)} %pad.13.colvec, ...), custom_call_target="tpu_custom_call" | custom-call | tf_op jit(solution)/shard_map/pallas_call | solution.py:392
  154.3 1.3 copy.23
  155.6 3.2 %copy.25 = bf16[1,512,2048]{2,1,0:T(8,128)(2,1)} copy(bf16[1,512,2048]{2,1,0:T(8,128)(2,1)} %bitcast.23) | data formatting | bytes 4194304
  (3 shorter events, 0.0 us)

commit v3 on v2

--- a/solution.py
+++ b/solution.py
@@ -113,14 +113,15 @@
 NT = (((1,), (1,)), ((), ()))
 
 
-def fused(norm, omega, hamil, meta, ranks, cc_inv, colvec, actvec, order, order_t,
+def fused(norm, omega, hamil, pp, phs, rcr, ccr, permr, sor,
           z_out, ob_out,
           part_o, part_h, scal_o, scal_h, meta1, meta2s, meta2, sorted_r,
           send_a, recv_a, send_l, recv_l, ladder, x_send, x_recv, acc, rights,
           bars, back_s, back_r, ob1, ob2, right_s,
+          send_y, recv_y, meta, cc_parts, cc_inv, colvec, order, order_t,
           p_send, p_recv, m1_send, m1_recv, m2_send, m2_recv, a_send, a_recv,
           l_send, l_recv, x_ss, x_rs, r_send, r_recv, b_send, b_recv,
-          o1_send, o1_recv, o2_send, o2_recv):
+          o1_send, o1_recv, o2_send, o2_recv, y_send, y_recv):
     chans, splits = ob2.shape[0], ob1.shape[0]
     height, breadth = omega.shape
     slots = height // chans
@@ -157,15 +158,39 @@
     split_loop(lambda p: greet(c, p))
     pl.semaphore_wait(barrier, chans + splits - 2)
 
+    copy_o = remote(omega, part_o, p_send.at[0], p_recv.at[0], c, partner)
+    copy_h = remote(hamil, part_h, p_send.at[1], p_recv.at[1], c, partner)
+    copy_o.start()
+    copy_h.start()
+
+    own_cols = pl.ds(pl.multiple_of(s * height, height), height)
+    down = lax.broadcasted_iota(jnp.int32, (height, height), 0)
+    over = lax.broadcasted_iota(jnp.int32, (height, height), 1)
+    mask = jnp.where(phs[...] != 0.0, 1.0, 0.0)
+    lower = jnp.where(down <= over, 1.0, 0.0).astype(BF16)
+    count = dot(jnp.broadcast_to(mask, (16, height)).astype(BF16), lower)[0:1]
+    rank = jnp.where(mask > 0.0, count - 1.0, -1.0)
+    lane_of = jnp.where(mask > 0.0, count - 1.0 + (s * active).astype(F32), -1.0)
+    pick = lax.broadcasted_iota(jnp.int32, (wide, height), 0).astype(F32)
+    pick = jnp.where(pick == lane_of, 1.0, 0.0)
+    meta[...] = jnp.zeros_like(meta)
+    meta[0:1, :] = permr[:, own_cols].astype(F32)
+    meta[1:2, :] = ccr[:, own_cols]
+    chosen = lax.dot_general(meta[...], pick, NT, precision=lax.Precision.HIGHEST,
+                             preferred_element_type=F32)
+    meta[0:2, :wide] = chosen[0:2]
+    meta[2:3, :] = pp[...]
+
     def m1(p, frm):
         return remote(meta, meta1.at[frm], m1_send.at[p], m1_recv.at[frm], c, p)
     split_loop(lambda p: m1(p, s).start())
     meta1[s] = meta[...]
 
-    copy_o = remote(omega, part_o, p_send.at[0], p_recv.at[0], c, partner)
-    copy_h = remote(hamil, part_h, p_send.at[1], p_recv.at[1], c, partner)
-    copy_o.start()
-    copy_h.start()
+    turned = jnp.where(down == sor[...], 1.0, 0.0)
+    order_t[...] = turned.astype(BF16)
+    order[...] = turned.T.astype(BF16)
+    colvec[:, 0:1] = jnp.sum(jnp.where(down == over, pp[...], 0.0), axis=1, keepdims=True)
+    colvec[:, 1:2] = jnp.sum(jnp.where(down == over, rcr[...], 0.0), axis=1, keepdims=True)
 
     tile = 256
     def sort_tile(n, carry):
@@ -181,7 +206,8 @@
     sums = meta1[0] + meta1[1] + meta1[2] + meta1[3]
     cols_row, act_cc = sums[0:1, :wide], sums[1:2, :wide]
     for q in range(chans):
-        meta2s[q] = ranks[q]
+        meta2s[q] = jnp.zeros(meta2s.shape[1:], F32)
+        meta2s[q, 1:2, :slots] = rank[:, q * slots : (q + 1) * slots]
         meta2s[q, 0:1, :] = cols_row
 
     def m2(q, frm):
@@ -189,29 +215,61 @@
     chan_loop(lambda q: m2(q, c).start())
     meta2[c] = meta2s[c]
 
-    def copy_a(q, frm):
-        return remote(send_a.at[q], recv_a.at[frm], a_send.at[q], a_recv.at[frm], q, s)
+    rungs = chans // 2
+    z, y = c // 2, lax.rem(c, 2)
+
+    def copy_y(to):
+        return remote(send_y.at[to], recv_y.at[to], y_send.at[to], y_recv.at[to],
+                      z * 2 + 1 - y, s)
+
+    def copy_a(to, frm):
+        return remote(send_a.at[to], recv_a.at[frm], a_send.at[to], a_recv.at[frm],
+                      to * 2 + y, s)
 
     def copy_l(q, frm):
         return remote(send_l.at[q], recv_l.at[frm], l_send.at[q], l_recv.at[frm], q, s)
 
-    def pack(q, rows_to, left_to):
-        want = meta2[q]
+    def pack_rows(q):
         take = lax.broadcasted_iota(jnp.int32, (active, slots), 0).astype(F32)
-        take = jnp.where(take == want[1:2, :slots], 1.0, 0.0).astype(BF16)
-        rows_to[q, :active] = dot(take, sorted_r[q, :slots]).astype(BF16)
-        rows_to[q, active:] = dot(take, sorted_r[q, slots:]).astype(BF16)
+        take = jnp.where(take == meta2[q, 1:2, :slots], 1.0, 0.0).astype(BF16)
+        return dot(take, sorted_r[q, :slots]), dot(take, sorted_r[q, slots:])
+
+    def pack_left(q, to):
         gate = lax.broadcasted_iota(jnp.int32, (breadth, wide), 0).astype(F32)
-        gate = jnp.where(gate == want[0:1, :wide], 1.0, 0.0).astype(BF16)
-        left_to[q] = dot(sorted_r[q], gate).astype(BF16)
-
-    def pack_send(q):
+        gate = jnp.where(gate == meta2[q, 0:1, :wide], 1.0, 0.0).astype(BF16)
+        to[q] = dot(sorted_r[q], gate).astype(BF16)
+
+    def to_side(d, carry):
+        to = lax.rem(z + 1 + d, rungs)
+        q = to * 2 + 1 - y
         m2(q, q).wait_recv()
-        pack(q, send_a, send_l)
-        copy_a(q, c).start()
+        got_o, got_h = pack_rows(q)
+        send_y[to, :active] = got_o.astype(BF16)
+        send_y[to, active:] = got_h.astype(BF16)
+        copy_y(to).start()
+        return carry
+    lax.fori_loop(0, rungs, to_side, 0)
+
+    def along(to, out):
+        got_o, got_h = pack_rows(to * 2 + y)
+        copy_y(to).wait_recv()
+        out[to, :active] = (got_o + recv_y[to, :active].astype(F32)).astype(BF16)
+        out[to, active:] = (got_h + recv_y[to, active:].astype(F32)).astype(BF16)
+
+    def along_send(d, carry):
+        to = lax.rem(z + 1 + d, rungs)
+        m2(to * 2 + y, to * 2 + y).wait_recv()
+        along(to, send_a)
+        copy_a(to, z).start()
+        return carry
+    lax.fori_loop(0, rungs - 1, along_send, 0)
+
+    def left_send(q):
+        pack_left(q, send_l)
         copy_l(q, c).start()
-    chan_loop(pack_send)
-    pack(c, recv_a, recv_l)
+    chan_loop(left_send)
+    pack_left(c, recv_l)
+    along(z, recv_a)
 
     span = height
     for k in range(splits):
@@ -252,23 +310,48 @@
         return carry
     lax.fori_loop(0, span // tile, same, 0)
 
-    acc[...] = recv_a[c].astype(F32)
-
-    def add_rows(q):
-        copy_a(q, q).wait_recv()
-        acc[...] += recv_a[q].astype(F32)
-    chan_loop(add_rows)
-    coef_a = actvec[:, 0:1] * cc_inv[...]
-    signs = actvec[:, 1:2]
+    cc_parts[...] = jnp.zeros_like(cc_parts)
+    first = ccr[...].astype(BF16).astype(F32)
+    second = (ccr[...] - first).astype(BF16).astype(F32)
+    third = ccr[...] - first - second
+    cc_parts[0:1, :] = first
+    cc_parts[1:2, :] = second
+    cc_parts[2:3, :] = third
+
+    def invert(n, carry):
+        hit = lax.broadcasted_iota(jnp.int32, (tile, breadth), 0) + n * tile
+        hit = jnp.where(hit == permr[...], 1.0, 0.0).astype(BF16)
+        val = lax.dot_general(cc_parts[...].astype(BF16), hit, NT, preferred_element_type=F32)
+        cc_inv[:, pl.ds(pl.multiple_of(n * tile, tile), tile)] = jnp.sum(
+            val, axis=0, keepdims=True)
+        return carry
+    lax.fori_loop(0, breadth // tile, invert, 0)
+    slot_of = lax.broadcasted_iota(jnp.int32, (active, height), 0).astype(F32)
+    act_rc = jnp.sum(jnp.where(slot_of == rank, rcr[...], 0.0), axis=1, keepdims=True)
+    signs = jnp.sum(jnp.where(slot_of == rank, phs[...], 0.0), axis=1, keepdims=True)
+
+    acc[...] = recv_a[z].astype(F32)
+
+    def add_rows(d, carry):
+        frm = lax.rem(z + 1 + d, rungs)
+        copy_a(frm, frm).wait_recv()
+        acc[...] += recv_a[frm].astype(F32)
+        return carry
+    lax.fori_loop(0, rungs - 1, add_rows, 0)
+    coef_a = act_rc * cc_inv[...]
     right_s[1] = (-signs * (coef_a * acc[:active]).astype(BF16).astype(F32)).astype(BF16)
     right_s[0] = (signs * (coef_a * acc[active:]).astype(BF16).astype(F32)).astype(BF16)
 
     def place(p):
         return rights.at[:, pl.ds(pl.multiple_of(p * active, active), active), :]
 
-    def copy_r(p, frm):
-        return remote(right_s, place(frm), r_send.at[p], r_recv.at[frm], c, p)
-    split_loop(lambda p: copy_r(p, s).start())
+    away = lax.rem(s + 2, splits)
+    partner_away = lax.rem(partner + 2, splits)
+
+    def copy_r(src, block, p, which):
+        return remote(src, place(block), r_send.at[which], r_recv.at[block], c, p)
+    copy_r(right_s, s, away, 0).start()
+    copy_r(right_s, s, partner, 1).start()
     rights[:, pl.ds(pl.multiple_of(s * active, active), active), :] = right_s[...]
 
     def make_bars(q):
@@ -282,7 +365,10 @@
         make_bars(q)
     chan_loop(bars_from)
     make_bars(c)
-    split_loop(lambda p: copy_r(p, p).wait_recv())
+    copy_r(right_s, away, away, 0).wait_recv()
+    copy_r(place(away), away, partner, 2).start()
+    copy_r(right_s, partner, partner, 1).wait_recv()
+    copy_r(right_s, partner_away, partner, 2).wait_recv()
 
     def copy_b(q, frm):
         return remote(back_s.at[q], back_r.at[frm], b_send.at[q], b_recv.at[frm], q, s)
@@ -336,7 +422,9 @@
     ob_out[...] = whole * norm
 
     split_loop(lambda p: m1(p, s).wait_send())
-    split_loop(lambda p: copy_r(p, s).wait_send())
+    copy_r(right_s, s, away, 0).wait_send()
+    copy_r(right_s, s, partner, 1).wait_send()
+    copy_r(place(away), away, partner, 2).wait_send()
     split_loop(lambda p: copy_o1(p, s).wait_send())
     copy_o.wait_send()
     copy_h.wait_send()
@@ -345,11 +433,20 @@
 
     def sent(q):
         m2(q, c).wait_send()
-        copy_a(q, c).wait_send()
         copy_l(q, c).wait_send()
         copy_b(q, c).wait_send()
         copy_o2(q, c).wait_send()
     chan_loop(sent)
+
+    def sent_rows(d, carry):
+        copy_a(lax.rem(z + 1 + d, rungs), z).wait_send()
+        return carry
+    lax.fori_loop(0, rungs - 1, sent_rows, 0)
+
+    def sent_side(d, carry):
+        copy_y(d).wait_send()
+        return carry
+    lax.fori_loop(0, rungs, sent_side, 0)
 
 
 def on_device_fused(omega, hamil, pp_sign, ph_sign, row_coef, col_coef, col_perm, send_order):
@@ -357,34 +454,7 @@
     _, height, breadth = omega.shape
     slots, active = height // chans, height // 16
     wide = active * splits
-    me_s = lax.axis_index("split")
-    sign = ph_sign[0]
-    mask = sign != 0
-    lower = jnp.arange(height)[:, None] <= jnp.arange(height)[None, :]
-    rank = jnp.sum(jnp.where(lower & mask[:, None], 1, 0), axis=0) - 1
-    rank = jnp.where(mask, rank, -1)
-    own_perm = lax.dynamic_slice(col_perm[0], (me_s * height,), (height,)).astype(F32)
-    own_cc = lax.dynamic_slice(col_coef[0], (me_s * height,), (height,))
-    lanes = jnp.arange(height)
-    pick = (rank[:, None] + me_s * active == lanes[None, :]) & mask[:, None]
-
-    def picked(values):
-        return jnp.sum(jnp.where(pick, values[:, None], 0.0), axis=0)
-    pad = jnp.zeros((5, height), F32)
-    meta = jnp.concatenate(
-        [picked(own_perm)[None], picked(own_cc)[None], pp_sign[0][None], pad])
-    ranks = jnp.pad(rank.astype(F32).reshape(chans, 1, slots),
-                    ((0, 0), (1, 6), (0, wide - slots)), constant_values=-1.0)
-    hit = col_perm[0][:, None] == jnp.arange(breadth)[None, :]
-    cc_inv = jnp.sum(jnp.where(hit, col_coef[0][:, None], 0.0), axis=0)[None]
-    colvec = jnp.stack([pp_sign[0], row_coef[0]], axis=1)
-    colvec = jnp.pad(colvec, ((0, 0), (0, 126)))
-    pick_a = rank[None, :] == jnp.arange(active)[:, None]
-    actvec = jnp.stack([jnp.sum(jnp.where(pick_a, v[None, :], 0.0), axis=1)
-                        for v in (row_coef[0], sign)], axis=1)
-    actvec = jnp.pad(actvec, ((0, 0), (0, 126)))
-    order = (send_order[0][:, None] == lanes[None, :]).astype(BF16)
-    order_t = (send_order[0][None, :] == lanes[:, None]).astype(BF16)
+    rungs = chans // 2
     weight_sq = sum((2 * (i // 2) + 1) ** 2 for i in range(chans))
     norm = 1.0 / math.sqrt(breadth * weight_sq)
     vm = pl.BlockSpec(memory_space=pltpu.VMEM)
@@ -393,7 +463,7 @@
         functools.partial(fused, norm),
         out_shape=(jax.ShapeDtypeStruct((height, breadth), BF16),
                    jax.ShapeDtypeStruct((8, breadth // 8), F32)),
-        in_specs=[vm] * 9,
+        in_specs=[vm] * 8,
         out_specs=(vm, vm),
         scratch_shapes=[
             pltpu.VMEM((height, breadth), BF16), pltpu.VMEM((height, breadth), BF16),
@@ -401,8 +471,8 @@
             pltpu.VMEM((splits, 8, height), F32),
             pltpu.VMEM((chans, 8, wide), F32), pltpu.VMEM((chans, 8, wide), F32),
             pltpu.VMEM((chans, 2 * slots, breadth), BF16),
-            pltpu.VMEM((chans, 2 * active, breadth), BF16),
-            pltpu.VMEM((chans, 2 * active, breadth), BF16),
+            pltpu.VMEM((rungs, 2 * active, breadth), BF16),
+            pltpu.VMEM((rungs, 2 * active, breadth), BF16),
             pltpu.VMEM((chans, 2 * slots, wide), BF16),
             pltpu.VMEM((chans, 2 * slots, wide), BF16),
             pltpu.VMEM((height, breadth), F32),
@@ -415,15 +485,23 @@
             pltpu.VMEM((splits, 8, breadth // 8), F32),
             pltpu.VMEM((chans, 8, breadth // 8), F32),
             pltpu.VMEM((2, active, breadth), BF16),
+            pltpu.VMEM((rungs, 2 * active, breadth), BF16),
+            pltpu.VMEM((rungs, 2 * active, breadth), BF16),
+            pltpu.VMEM((8, height), F32),
+            pltpu.VMEM((16, breadth), F32),
+            pltpu.VMEM((1, breadth), F32),
+            pltpu.VMEM((height, 128), F32),
+            pltpu.VMEM((height, height), BF16), pltpu.VMEM((height, height), BF16),
             dma((2,)), dma((2,)), dma((splits,)), dma((splits,)),
             dma((chans,)), dma((chans,)), dma((chans,)), dma((chans,)),
             dma((chans,)), dma((chans,)), dma((2,)), dma((2,)),
             dma((splits,)), dma((splits,)), dma((chans,)), dma((chans,)),
             dma((splits,)), dma((splits,)), dma((chans,)), dma((chans,)),
+            dma((rungs,)), dma((rungs,)),
         ],
         compiler_params=pltpu.CompilerParams(
             collective_id=0, has_side_effects=True, vmem_limit_bytes=58 * 2**20),
-    )(omega[0], hamil[0], meta, ranks, cc_inv, colvec, actvec, order, order_t)
+    )(omega[0], hamil[0], pp_sign, ph_sign, row_coef, col_coef, col_perm, send_order)
     return z_out[None], one_body.reshape(-1)
 
 

time: 159 us -> 143 us (0.90)
  other arithmetic: 12.6 us -> 0 us
  local copies, waits for them, and re-layouts: 7.56 us -> 4.46 us
    reduce_sum x4 -> x0, other arithmetic: 5.19 us -> none  [the longest x1 3.86 us: on_device_fused(): cc_inv = jnp.sum(jnp.where(hit, col_coef[0][:, None], 0.0), axis=0)[None]]
    convert_element_type x3 -> x0, other arithmetic: 2.57 us -> none  [the longest x1 1.88 us: on_device_fused(): order_t = (send_order[0][None, :] == lanes[:, None]).astype(BF16)]
    pad x3 -> x0, local copies, waits for them, and re-layouts: 1.94 us -> none  [the longest x1 0.73 us: on_device_fused(): colvec = jnp.pad(colvec, ((0, 0), (0, 126)))]
where the time goes in v3:
time: 143 us
  Pallas kernels  137 us (96%)
  local copies, waits for them, and re-layouts  4.46 us (3%)
    pallas_call x1, Pallas kernels, on_device_fused(): pl.pallas_call(functools.partial(fused, norm), out_shape=(jax.ShapeDtypeS...  137 us
    unnamed x2, local copies, waits for them, and re-layouts  4.46 us

profile of v3, /device:TPU:0, one launch (start us, length us, event | category | flops | bytes accessed | tf_op | source)
XLA Modules:
  0.0 142.6 jit_solution(6234191577615362441)
XLA Ops:
  0.6 137.5 %shard_map.95 = (bf16[512,2048]{1,0:T(8,128)(2,1)}, f32[8,256]{1,0:T(8,128)}) custom-call(bf16[512,2048]{1,0:T(8,128)(2,1)} %bitcast.5, bf16[512,2048]{1,0:T(8,128)(2,1)} %bitcast.6, f32[1,512]{1,0:T(1,128)} %pp.1, f32[1,512]{1,0:T(1,128)} %phs.1, f32[1,512]{1,0:T(1,128)} %rcr.1, f32[1,2048]{1,0:T(1,128)} %ccr.1, s32[1,2048]{1,0:T(1,128)} %permr.1, s32[1,512]{1,0:T(1,128)} %sor.1), custom_call_target="tpu_custom_call" | custom-call | tf_op jit(solution)/shard_map/pallas_call | solution.py:462
  138.1 1.3 copy.10
  139.4 3.2 %copy.12 = bf16[1,512,2048]{2,1,0:T(8,128)(2,1)} copy(bf16[1,512,2048]{2,1,0:T(8,128)(2,1)} %bitcast.7) | data formatting | bytes 4194304

commit v4 on v3

--- a/solution.py
+++ b/solution.py
@@ -277,6 +277,81 @@
         sgn = meta1[k, 2:3, :]
         scal_o[:, cols] = (omega[:, cols].astype(F32) * sgn).astype(BF16)
         scal_h[:, cols] = (hamil[:, cols].astype(F32) * sgn).astype(BF16)
+
+    cc_parts[...] = jnp.zeros_like(cc_parts)
+    first = ccr[...].astype(BF16).astype(F32)
+    second = (ccr[...] - first).astype(BF16).astype(F32)
+    third = ccr[...] - first - second
+    cc_parts[0:1, :] = first
+    cc_parts[1:2, :] = second
+    cc_parts[2:3, :] = third
+
+    def invert(n, carry):
+        hit = lax.broadcasted_iota(jnp.int32, (tile, breadth), 0) + n * tile
+        hit = jnp.where(hit == permr[...], 1.0, 0.0).astype(BF16)
+        val = lax.dot_general(cc_parts[...].astype(BF16), hit, NT, preferred_element_type=F32)
+        cc_inv[:, pl.ds(pl.multiple_of(n * tile, tile), tile)] = jnp.sum(
+            val, axis=0, keepdims=True)
+        return carry
+    lax.fori_loop(0, breadth // tile, invert, 0)
+    slot_of = lax.broadcasted_iota(jnp.int32, (active, height), 0).astype(F32)
+    act_rc = jnp.sum(jnp.where(slot_of == rank, rcr[...], 0.0), axis=1, keepdims=True)
+    signs = jnp.sum(jnp.where(slot_of == rank, phs[...], 0.0), axis=1, keepdims=True)
+
+    acc[...] = recv_a[z].astype(F32)
+
+    def add_rows(d, carry):
+        frm = lax.rem(z + 1 + d, rungs)
+        copy_a(frm, frm).wait_recv()
+        acc[...] += recv_a[frm].astype(F32)
+        return carry
+    lax.fori_loop(0, rungs - 1, add_rows, 0)
+    coef_a = act_rc * cc_inv[...]
+    right_s[1] = (-signs * (coef_a * acc[:active]).astype(BF16).astype(F32)).astype(BF16)
+    right_s[0] = (signs * (coef_a * acc[active:]).astype(BF16).astype(F32)).astype(BF16)
+
+    def place(p):
+        return rights.at[:, pl.ds(pl.multiple_of(p * active, active), active), :]
+
+    away = lax.rem(s + 2, splits)
+    partner_away = lax.rem(partner + 2, splits)
+
+    def copy_r(src, block, p, which):
+        return remote(src, place(block), r_send.at[which], r_recv.at[block], c, p)
+    copy_r(right_s, s, away, 0).start()
+    copy_r(right_s, s, partner, 1).start()
+    rights[:, pl.ds(pl.multiple_of(s * active, active), active), :] = right_s[...]
+
+    def make_bars(q):
+        rows = pl.ds(pl.multiple_of(q * slots, slots), slots)
+        coef = colvec[rows, 1:2] * act_cc
+        bars[rows, :wide] = (coef * recv_l[q, :slots].astype(F32)).astype(BF16)
+        bars[rows, wide:] = (coef * recv_l[q, slots:].astype(F32)).astype(BF16)
+
+    def bars_from(q):
+        copy_l(q, q).wait_recv()
+        make_bars(q)
+    chan_loop(bars_from)
+    make_bars(c)
+    copy_r(right_s, away, away, 0).wait_recv()
+    copy_r(place(away), away, partner, 2).start()
+    copy_r(right_s, partner, partner, 1).wait_recv()
+    copy_r(right_s, partner_away, partner, 2).wait_recv()
+
+    def copy_b(q, frm):
+        return remote(back_s.at[q], back_r.at[frm], b_send.at[q], b_recv.at[frm], q, s)
+
+    def product(q, to):
+        rows = pl.ds(pl.multiple_of(q * slots, slots), slots)
+        val = dot(bars[rows, :wide], rights[0]) + dot(bars[rows, wide:], rights[1])
+        to[q] = (colvec[rows, 1:2] * cc_inv[...] * val).astype(BF16)
+
+    def product_send(q):
+        product(q, back_s)
+        copy_b(q, c).start()
+    chan_loop(product_send)
+    product(c, back_r)
+
     copy_o.wait_recv()
     copy_h.wait_recv()
     own = pl.ds(pl.multiple_of(s * span, span), span)
@@ -309,80 +384,6 @@
         ladder[:, pl.ds(pl.multiple_of(s * span + t * tile, tile), tile)] = val
         return carry
     lax.fori_loop(0, span // tile, same, 0)
-
-    cc_parts[...] = jnp.zeros_like(cc_parts)
-    first = ccr[...].astype(BF16).astype(F32)
-    second = (ccr[...] - first).astype(BF16).astype(F32)
-    third = ccr[...] - first - second
-    cc_parts[0:1, :] = first
-    cc_parts[1:2, :] = second
-    cc_parts[2:3, :] = third
-
-    def invert(n, carry):
-        hit = lax.broadcasted_iota(jnp.int32, (tile, breadth), 0) + n * tile
-        hit = jnp.where(hit == permr[...], 1.0, 0.0).astype(BF16)
-        val = lax.dot_general(cc_parts[...].astype(BF16), hit, NT, preferred_element_type=F32)
-        cc_inv[:, pl.ds(pl.multiple_of(n * tile, tile), tile)] = jnp.sum(
-            val, axis=0, keepdims=True)
-        return carry
-    lax.fori_loop(0, breadth // tile, invert, 0)
-    slot_of = lax.broadcasted_iota(jnp.int32, (active, height), 0).astype(F32)
-    act_rc = jnp.sum(jnp.where(slot_of == rank, rcr[...], 0.0), axis=1, keepdims=True)
-    signs = jnp.sum(jnp.where(slot_of == rank, phs[...], 0.0), axis=1, keepdims=True)
-
-    acc[...] = recv_a[z].astype(F32)
-
-    def add_rows(d, carry):
-        frm = lax.rem(z + 1 + d, rungs)
-        copy_a(frm, frm).wait_recv()
-        acc[...] += recv_a[frm].astype(F32)
-        return carry
-    lax.fori_loop(0, rungs - 1, add_rows, 0)
-    coef_a = act_rc * cc_inv[...]
-    right_s[1] = (-signs * (coef_a * acc[:active]).astype(BF16).astype(F32)).astype(BF16)
-    right_s[0] = (signs * (coef_a * acc[active:]).astype(BF16).astype(F32)).astype(BF16)
-
-    def place(p):
-        return rights.at[:, pl.ds(pl.multiple_of(p * active, active), active), :]
-
-    away = lax.rem(s + 2, splits)
-    partner_away = lax.rem(partner + 2, splits)
-
-    def copy_r(src, block, p, which):
-        return remote(src, place(block), r_send.at[which], r_recv.at[block], c, p)
-    copy_r(right_s, s, away, 0).start()
-    copy_r(right_s, s, partner, 1).start()
-    rights[:, pl.ds(pl.multiple_of(s * active, active), active), :] = right_s[...]
-
-    def make_bars(q):
-        rows = pl.ds(pl.multiple_of(q * slots, slots), slots)
-        coef = colvec[rows, 1:2] * act_cc
-        bars[rows, :wide] = (coef * recv_l[q, :slots].astype(F32)).astype(BF16)
-        bars[rows, wide:] = (coef * recv_l[q, slots:].astype(F32)).astype(BF16)
-
-    def bars_from(q):
-        copy_l(q, q).wait_recv()
-        make_bars(q)
-    chan_loop(bars_from)
-    make_bars(c)
-    copy_r(right_s, away, away, 0).wait_recv()
-    copy_r(place(away), away, partner, 2).start()
-    copy_r(right_s, partner, partner, 1).wait_recv()
-    copy_r(right_s, partner_away, partner, 2).wait_recv()
-
-    def copy_b(q, frm):
-        return remote(back_s.at[q], back_r.at[frm], b_send.at[q], b_recv.at[frm], q, s)
-
-    def product(q, to):
-        rows = pl.ds(pl.multiple_of(q * slots, slots), slots)
-        val = dot(bars[rows, :wide], rights[0]) + dot(bars[rows, wide:], rights[1])
-        to[q] = (colvec[rows, 1:2] * cc_inv[...] * val).astype(BF16)
-
-    def product_send(q):
-        product(q, back_s)
-        copy_b(q, c).start()
-    chan_loop(product_send)
-    product(c, back_r)
 
     for m in range(2):
         copy_x(m, m).wait_recv()

time: 143 us -> 130 us (0.909)
  Pallas kernels: 137 us -> 125 us
    pallas_call x1, Pallas kernels: 137 us -> 125 us  [on_device_fused(): pl.pallas_call(functools.partial(fused, norm), out_shape=(jax.ShapeDtypeS...]
where the time goes in v4:
time: 130 us
  Pallas kernels  125 us (96%)
  local copies, waits for them, and re-layouts  4.46 us (3%)
    pallas_call x1, Pallas kernels, on_device_fused(): pl.pallas_call(functools.partial(fused, norm), out_shape=(jax.ShapeDtypeS...  125 us
    unnamed x2, local copies, waits for them, and re-layouts  4.46 us

profile of v4, /device:TPU:0, one launch (start us, length us, event | category | flops | bytes accessed | tf_op | source)
XLA Modules:
  0.0 129.7 jit_solution(5591088075552596641)
XLA Ops:
  0.6 124.6 %shard_map.95 = (bf16[512,2048]{1,0:T(8,128)(2,1)}, f32[8,256]{1,0:T(8,128)}) custom-call(bf16[512,2048]{1,0:T(8,128)(2,1)} %bitcast.5, bf16[512,2048]{1,0:T(8,128)(2,1)} %bitcast.6, f32[1,512]{1,0:T(1,128)} %pp.1, f32[1,512]{1,0:T(1,128)} %phs.1, f32[1,512]{1,0:T(1,128)} %rcr.1, f32[1,2048]{1,0:T(1,128)} %ccr.1, s32[1,2048]{1,0:T(1,128)} %permr.1, s32[1,512]{1,0:T(1,128)} %sor.1), custom_call_target="tpu_custom_call" | custom-call | tf_op jit(solution)/shard_map/pallas_call | solution.py:463
  125.2 1.3 %copy.10 = f32[1,2,8,128]{3,1,2,0:T(2,128)} copy(f32[1,2,8,128]{3,2,1,0:T(8,128)} %bitcast.9) | data formatting | bytes 16384
  126.5 3.2 %copy.12 = bf16[1,512,2048]{2,1,0:T(8,128)(2,1)} copy(bf16[1,512,2048]{2,1,0:T(8,128)(2,1)} %bitcast.7) | data formatting | bytes 4194304
